TPU v7x, 32 devices: a whole 2x2x4 slice. The times are simulated.
32 devices in a mesh: groups: 2 (over x), users: 16 (over z, y, core).
Axes of the slice: x: 2, y: 2, z: 4, core: 2. Of those that a mesh axis runs over, the one named last changes fastest.
Arguments:
- history: bfloat16 [32, 512, 1024], P(('groups', 'users')), parts along dimension 0, may hold values from -6 to 6
- hist_len: int32 [32], P(('groups', 'users')), parts along dimension 0, may hold values from 128 to 512, as said below
- candidates: bfloat16 [8192, 1024], P(('groups', 'users')), parts along dimension 0, may hold values from -6 to 6
- cand_user: int32 [8192, 1], P(('groups', 'users')), parts along dimension 0, may hold values from 0 to 15; in each aligned block of 256 rows (0 to 255, 256 to 511, ...) at most 32 rows name the same one
- cand_task: int32 [8192], P(('groups', 'users')), parts along dimension 0, may hold values from 0 to 2
- kv_weight: bfloat16 [1024, 2048], replicated, may hold values from -1 to 1
- query_weight: bfloat16 [1024, 1024], replicated, may hold values from -1 to 1
- out_weight: bfloat16 [1024, 1024], replicated, may hold values from -0.75 to 0.75
- head_weight: bfloat16 [1024, 3], replicated, may hold values from -0.1875 to 0.1875
Outputs:
- new_history: bfloat16 [32, 512, 1024], P(('groups', 'users')), parts along dimension 0
- scores: float32 [8192], P(('groups', 'users')), parts along dimension 0
There are 2 independent parts, one for each index of `groups`. A program takes and returns all parts, laid end to end along the dimension named above; an argument that names none is the same for every part. Nothing has to cross between parts.
Inputs may be any that keep to these rules, and one draw needn't show every extreme that they name: `hist_len`: each history holds a whole number of pages of 128 events, and some user has all 512. `cand_user`: among the slots of one device no user is named more than 32 times; on some device some user is named exactly 32 times.
All inputs are finite; a program needn't handle non-finite values.
Results may differ from a plain program's by a relative error of at most 0.012.
The roundings to bfloat16 on the way count: a program that leaves them out, or rounds other values in their place, can miss the bound.
Values may be sent and summed in bfloat16 or wider, within the bound.
A program may use at most 192 MiB of HBM per device.

v0:
```python
import jax
import jax.numpy as jnp
from jax import lax
from jax.sharding import PartitionSpec as P

HEADS = 16


epsilon = 1e-06


def normalize(values):
    values = values.astype(jnp.float32)
    return values * lax.rsqrt(jnp.mean(values * values, axis=-1, keepdims=True) + epsilon)


def attend(queries, key_rows, value_rows, allowed):
    query_count = queries.shape[0]
    events = key_rows.shape[0]
    head_size = queries.shape[1] // HEADS
    query_heads = queries.reshape(query_count, HEADS, head_size)
    key_heads = key_rows.reshape(events, HEADS, head_size)
    value_heads = value_rows.reshape(events, HEADS, head_size)
    scores = jnp.einsum(
        "rhd,khd->hrk", query_heads, key_heads, preferred_element_type=jnp.float32
    ) * head_size ** (-0.5)
    scores = jnp.where(allowed[None, :, :], scores, -jnp.inf)
    highest = jnp.max(scores, axis=-1, keepdims=True)
    raised = jnp.exp(scores - highest)
    weights = (raised / jnp.sum(raised, axis=-1, keepdims=True)).astype(jnp.bfloat16)
    context = jnp.einsum("hrk,khd->rhd", weights, value_heads, preferred_element_type=jnp.float32)
    return context.reshape(query_count, HEADS * head_size).astype(jnp.bfloat16)


def on_device(
    history,
    hist_len,
    candidates,
    cand_user,
    cand_task,
    kv_weight,
    query_weight,
    out_weight,
    head_weight,
):
    peer_count = lax.axis_size("users")
    slot_count = candidates.shape[0]
    per_owner = 2 * slot_count // peer_count
    features = candidates.shape[1]
    user_events = history[0]
    length = hist_len[0]
    events = user_events.shape[0]
    normed = normalize(user_events).astype(jnp.bfloat16)
    joined_kv = jnp.dot(normed, kv_weight, preferred_element_type=jnp.float32).astype(jnp.bfloat16)
    key_rows = joined_kv[:, :features]
    value_rows = joined_kv[:, features:]
    history_queries = jnp.dot(normed, query_weight, preferred_element_type=jnp.float32).astype(
        jnp.bfloat16
    )
    position = jnp.arange(events)
    causal = (position[None, :] <= position[:, None]) & (position[None, :] < length)
    owners = cand_user[:, 0]
    matches = (owners[:, None] == jnp.arange(peer_count)[None, :]).astype(jnp.int32)
    within = jnp.sum(jnp.cumsum(matches, axis=0) * matches, axis=1) - 1
    target = owners * per_owner + within
    cand_queries = jnp.dot(
        normalize(candidates).astype(jnp.bfloat16), query_weight, preferred_element_type=jnp.float32
    ).astype(jnp.bfloat16)
    blank_slots = jnp.zeros((peer_count * per_owner, cand_queries.shape[1]), cand_queries.dtype)
    arrived = lax.all_to_all(
        blank_slots.at[target]
        .set(cand_queries)
        .reshape(peer_count, per_owner, cand_queries.shape[1]),
        "users",
        split_axis=0,
        concat_axis=0,
        tiled=True,
    )
    arrived = arrived.reshape(peer_count * per_owner, features)
    visible = jnp.broadcast_to(position[None, :] < length, (arrived.shape[0], events))
    context = attend(
        jnp.concatenate([history_queries, arrived], axis=0),
        key_rows,
        value_rows,
        jnp.concatenate([causal, visible], axis=0),
    )
    history_context = context[:events]
    cand_context = context[events:]
    updated = user_events.astype(jnp.float32) + jnp.dot(
        history_context, out_weight, preferred_element_type=jnp.float32
    )
    updated = updated.astype(jnp.bfloat16)
    returned = lax.all_to_all(
        cand_context.reshape(peer_count, per_owner, features),
        "users",
        split_axis=0,
        concat_axis=0,
        tiled=True,
    )
    returned = returned.reshape(peer_count * per_owner, features)
    combined = candidates.astype(jnp.float32) + jnp.dot(
        returned[target], out_weight, preferred_element_type=jnp.float32
    )
    logits = jnp.dot(
        normalize(combined).astype(jnp.bfloat16), head_weight, preferred_element_type=jnp.float32
    )
    chosen = cand_task[:, None] == jnp.arange(logits.shape[1])[None, :]
    scores = jnp.sum(jnp.where(chosen, logits, jnp.zeros_like(logits)), axis=1)
    return (updated[None], scores)


def solution(mesh):
    placed = (
        P(("groups", "users"), None, None),
        P(("groups", "users")),
        P(("groups", "users"), None),
        P(("groups", "users"), None),
        P(("groups", "users")),
        P(),
        P(),
        P(),
        P(),
    )
    return jax.shard_map(
        on_device,
        mesh=mesh,
        in_specs=placed,
        out_specs=(P(("groups", "users"), None, None), P(("groups", "users"))),
        check_vma=False,
    )
```

profile of v0, /device:TPU:0, one launch (start us, length us, event | category | flops | bytes accessed | tf_op | source)
XLA Modules:
  0.0 152.9 jit_solution(16803559259366051533)
XLA Ops:
  0.6 0.8 fusion.27
  1.5 0.6 reduce-window.6
  2.0 0.2 slice_reduce_fusion
  2.3 0.8 fusion.26
  3.1 0.7 compare_select_fusion
  3.7 1.2 fusion.15
  5.0 2.5 %convolution_convert_fusion.2 = bf16[256,1024]{1,0:T(8,128)(2,1)S(1)} fusion(bf16[1024,1024]{1,0:T(8,128)(2,1)} %param.15, bf16[256,1024]{1,0:T(8,128)(2,1)} %param.11, f32[256]{0:T(256)S(1)} %add_rsqrt_fusion.2), kind=kOutput, calls=%fused_computation.29 | convolution fusion | flops 537919488 | bytes 3146752 | tf_op jit(solution)/shard_map/dot_general | solution.py:66
  7.5 2.7 %scatter_custom_fusion = bf16[512,1024]{1,0:T(8,128)(2,1)} fusion(s32[256]{0:T(256)S(1)} %bitcast.56, bf16[256,1024]{1,0:T(8,128)(2,1)S(1)} %convolution_convert_fusion.2, bf16[]{:T(256)} %constant.13.clone.1), kind=kCustom, calls=%fused_computation.40 | custom fusion | bytes 1048578 | tf_op jit(solution)/shard_map/scatter | solution.py:72
  10.2 7.4 %all-to-all-start = ((bf16[16,32,1024]{2,1,0:T(8,128)(2,1)}), bf16[16,32,1024]{2,1,0:T(8,128)(2,1)S(1)}, u32[]{:S(2)}, u32[]{:S(2)}) async-start(bf16[16,32,1024]{2,1,0:T(8,128)(2,1)} %bitcast.51), calls=%async_computation | async-start | bytes 2097152 | tf_op jit(solution)/shard_map/all_to_all | solution.py:70
  17.6 1.5 fusion.6
  19.1 4.9 %convolution_convert_fusion = bf16[512,2048]{1,0:T(8,128)(2,1)S(1)} fusion(bf16[1024,2048]{1,0:T(8,128)(2,1)} %param.14, bf16[1,512,1024]{2,1,0:T(8,128)(2,1)} %param.9, f32[512]{0:T(512)S(1)} %add_rsqrt_fusion), kind=kOutput, calls=%fused_computation.14 | convolution fusion | flops 2150105088 | bytes 7342080 | tf_op jit(solution)/shard_map/dot_general | solution.py:54
  24.0 1.5 fusion.32
  25.5 2.3 %copy.16 = bf16[512,1024]{0,1:T(8,128)(2,1)} copy(bf16[512,1024]{1,0:T(8,128)(2,1)} %get-tuple-element.5) | data formatting | bytes 2097152 | tf_op jit(solution)/shard_map/slice | solution.py:56
  27.8 2.3 %copy.20 = bf16[512,1024]{0,1:T(8,128)(2,1)} copy(bf16[512,1024]{1,0:T(8,128)(2,1)} %get-tuple-element.4) | data formatting | bytes 2097152 | tf_op jit(solution)/shard_map/slice | solution.py:55
  30.1 4.2 %convolution_convert_fusion.1 = bf16[512,1024]{1,0:T(8,128)(2,1)} fusion(bf16[1024,1024]{1,0:T(8,128)(2,1)} %param.15, bf16[1,512,1024]{2,1,0:T(8,128)(2,1)} %param.9, f32[512]{0:T(512)S(1)} %add_rsqrt_fusion), kind=kOutput, calls=%fused_computation.27 | convolution fusion | flops 1075838976 | bytes 4196352 | tf_op jit(solution)/shard_map/dot_general | solution.py:57
  34.3 2.3 %copy.17 = bf16[512,1024]{0,1:T(8,128)(2,1)} copy(bf16[512,1024]{1,0:T(8,128)(2,1)} %convolution_convert_fusion.1) | data formatting | bytes 2097152 | tf_op jit(solution)/shard_map/convert_element_type | solution.py:57
  37.5 0.8 pad_add_fusion
  38.4 2.2 %all-to-all-done = bf16[16,32,1024]{2,1,0:T(8,128)(2,1)S(1)} async-done(((bf16[16,32,1024]{2,1,0:T(8,128)(2,1)}), bf16[16,32,1024]{2,1,0:T(8,128)(2,1)S(1)}, u32[]{:S(2)}, u32[]{:S(2)}) %all-to-all-start) | async-done | bytes 1048608 | tf_op jit(solution)/shard_map/all_to_all | solution.py:70
  40.5 2.4 %concatenate.13 = bf16[512,16,64]{2,1,0:T(8,128)(2,1)} reshape(bf16[16,32,1024]{2,1,0:T(8,128)(2,1)S(1)} %all-to-all-done) | data formatting | bytes 2097152 | tf_op jit(solution)/shard_map/concatenate | solution.py:82
  42.9 2.5 %copy.19 = bf16[512,16,64]{0,2,1:T(8,128)(2,1)S(1)} copy(bf16[512,16,64]{2,1,0:T(8,128)(2,1)} %concatenate.13) | data formatting | bytes 2097152 | tf_op jit(solution)/shard_map/concatenate | solution.py:82
  45.4 17.2 %fusion.9 = f32[16,1024,512]{1,2,0:T(8,128)} fusion(bf16[512,16,64]{0,2,1:T(8,128)(2,1)} %bitcast.49, bf16[512,16,64]{0,2,1:T(8,128)(2,1)S(1)} %copy.19, bf16[512,16,64]{0,2,1:T(8,128)(2,1)} %bitcast.50), kind=kOutput, calls=%fused_computation.18 | convolution fusion | flops 1077936128 | bytes 36700160 | tf_op jit(solution)/shard_map/rhd,khd->hrk/dot_general | solution.py:24
  62.6 34.9 %fusion.33 = (f32[16,1024]{1,0:T(8,128)S(1)}, f32[16,1024,512]{1,2,0:T(8,128)}) fusion(f32[16,1024,512]{1,2,0:T(8,128)} %fusion.9, pred[1024,512]{0,1:T(8,128)(4,1)S(1)} %copy-done.2), kind=kOutput, calls=%fused_computation.63 | output fusion | flops 50332160 | bytes 67698688 | tf_op jit(solution)/shard_map/sub | solution.py:29
  97.5 12.4 %convert_bitcast_fusion = bf16[1024,16,64]{0,2,1:T(8,128)(2,1)S(1)} fusion(bf16[512,16,64]{0,2,1:T(8,128)(2,1)S(1)} %bitcast.52, f32[16,1024,512]{1,2,0:T(8,128)} %get-tuple-element.7, f32[16,1024]{1,0:T(8,128)S(1)} %get-tuple-element.6), kind=kOutput, calls=%fused_computation.22 | convolution fusion | flops 1091567616 | bytes 36765696 | tf_op jit(solution)/shard_map/hrk,khd->rhd/dot_general | solution.py:31
  109.9 1.2 fusion.31
  111.2 2.9 %copy.22 = bf16[512,16,64]{2,1,0:T(8,128)(2,1)} copy(bf16[512,16,64]{0,2,1:T(8,128)(2,1)S(1)} %get-tuple-element.2) | data formatting | bytes 2097152 | tf_op jit(solution)/shard_map/slice | solution.py:88
  114.1 4.1 %reshape.93 = bf16[16,32,1024]{2,1,0:T(8,128)(2,1)} reshape(bf16[512,16,64]{2,1,0:T(8,128)(2,1)} %copy.22) | data formatting | bytes 2097152 | tf_op jit(solution)/shard_map/reshape | solution.py:94
  118.2 6.9 %all-to-all-start.1 = ((bf16[16,32,1024]{2,1,0:T(8,128)(2,1)}), bf16[16,32,1024]{2,1,0:T(8,128)(2,1)S(1)}, u32[]{:S(2)}, u32[]{:S(2)}) async-start(bf16[16,32,1024]{2,1,0:T(8,128)(2,1)} %reshape.93), calls=%async_computation.1 | async-start | bytes 2097152 | tf_op jit(solution)/shard_map/all_to_all | solution.py:93
  125.1 3.8 %fusion.13 = bf16[1,512,1024]{2,1,0:T(8,128)(2,1)} fusion(bf16[512,1024]{0,1:T(8,128)(2,1)} %bitcast.53, bf16[1024,1024]{1,0:T(8,128)(2,1)S(1)} %copy-done, bf16[1,512,1024]{2,1,0:T(8,128)(2,1)} %param.9), kind=kOutput, calls=%fused_computation.28 | convolution fusion | flops 1075314688 | bytes 5242880 | tf_op jit(solution)/shard_map/dot_general | solution.py:89
  128.8 19.1 %all-to-all-done.1 = bf16[16,32,1024]{2,1,0:T(8,128)(2,1)S(1)} async-done(((bf16[16,32,1024]{2,1,0:T(8,128)(2,1)}), bf16[16,32,1024]{2,1,0:T(8,128)(2,1)S(1)}, u32[]{:S(2)}, u32[]{:S(2)}) %all-to-all-start.1) | async-done | bytes 1048608 | tf_op jit(solution)/shard_map/all_to_all | solution.py:93
  148.0 2.0 %gather_fusion = bf16[256,1024]{1,0:T(8,128)(2,1)} fusion(bf16[512,1024]{1,0:T(8,128)(2,1)S(1)} %bitcast.48, s32[1024]{0:T(1024)S(1)} %pad_clamp_fusion), kind=kCustom, calls=%fused_computation | custom fusion | bytes 1049600 | tf_op jit(solution)/shard_map/gather | solution.py:102
  149.9 2.0 %multiply_reduce_fusion = (f32[256]{0:T(256)S(1)}, f32[256,1024]{1,0:T(8,128)S(1)}) fusion(bf16[256,1024]{1,0:T(8,128)(2,1)} %gather_fusion, bf16[1024,1024]{1,0:T(8,128)(2,1)S(1)} %copy-done, bf16[256,1024]{1,0:T(8,128)(2,1)} %param.11), kind=kOutput, calls=%fused_computation.35 | convolution fusion | flops 537919232 | bytes 4195328 | tf_op jit(solution)/shard_map/dot_general | solution.py:101
  152.0 0.9 fusion.14
  (20 shorter events, 0.4 us)
Async XLA Ops:
  0.6 124.4 %copy-start = (bf16[1024,1024]{1,0:T(8,128)(2,1)S(1)}, bf16[1024,1024]{1,0:T(8,128)(2,1)}, u32[]{:S(2)}) copy-start(bf16[1024,1024]{1,0:T(8,128)(2,1)} %param.16) | copy-start | bytes 6291460
  10.2 30.3 %all-to-all-start = ((bf16[16,32,1024]{2,1,0:T(8,128)(2,1)}), bf16[16,32,1024]{2,1,0:T(8,128)(2,1)S(1)}, u32[]{:S(2)}, u32[]{:S(2)}) async-start(bf16[16,32,1024]{2,1,0:T(8,128)(2,1)} %bitcast.51), calls=%async_computation | async-start | bytes 2097152 | tf_op jit(solution)/shard_map/all_to_all | solution.py:70
  45.4 17.2 %copy-start.2 = (pred[1024,512]{0,1:T(8,128)(4,1)S(1)}, pred[1024,512]{0,1:T(8,128)(4,1)}, u32[]{:S(2)}) copy-start(pred[1024,512]{0,1:T(8,128)(4,1)} %pad_add_fusion) | copy-start | bytes 1572868
  62.6 34.9 %copy-start.1 = (bf16[512,1024]{0,1:T(8,128)(2,1)S(1)}, bf16[512,1024]{0,1:T(8,128)(2,1)}, u32[]{:S(2)}) copy-start(bf16[512,1024]{0,1:T(8,128)(2,1)} %copy.16) | copy-start | bytes 3145732
  118.2 29.8 %all-to-all-start.1 = ((bf16[16,32,1024]{2,1,0:T(8,128)(2,1)}), bf16[16,32,1024]{2,1,0:T(8,128)(2,1)S(1)}, u32[]{:S(2)}, u32[]{:S(2)}) async-start(bf16[16,32,1024]{2,1,0:T(8,128)(2,1)} %reshape.93), calls=%async_computation.1 | async-start | bytes 2097152 | tf_op jit(solution)/shard_map/all_to_all | solution.py:93
  149.9 2.0 %copy-start.3 = (bf16[1024,3]{0,1:T(4,128)(2,1)S(1)}, bf16[1024,3]{0,1:T(4,128)(2,1)}, u32[]{:S(2)}) copy-start(bf16[1024,3]{0,1:T(4,128)(2,1)} %param.17) | copy-start | bytes 18436
  149.9 2.1 %copy-start.4 = (s32[256]{0:T(256)S(1)}, s32[256]{0:T(256)}, u32[]{:S(2)}) copy-start(s32[256]{0:T(256)} %param.13) | copy-start | bytes 3076
where the time goes:
time: 155 us; the launch traced here: 153 us
  matrix products  48 us (31%)
  other arithmetic  41.5 us (27%)
  local copies, waits for them, and re-layouts  26.5 us (17%)
  waiting for transfers between devices  21.3 us (14%)
  starting transfers between devices  14.2 us (9%)
    sub x1, other arithmetic, attend(): raised = jnp.exp(scores - highest)  34.9 us
    all_to_all x1, waiting for transfers between devices, on_device(): lax.all_to_all(cand_context.reshape(peer_count, per_owner, features), 'us...  19.1 us
    dot_general x1, matrix products, attend(): jnp.einsum('rhd,khd->hrk', query_heads, key_heads, preferred_element_type...  17.2 us
    dot_general x1, matrix products, attend(): jnp.einsum('hrk,khd->rhd', weights, value_heads, preferred_element_type=j...  12.4 us
    all_to_all x1, starting transfers between devices, on_device(): lax.all_to_all(blank_slots.at[target].set(cand_queries).reshape(peer_coun...  7.37 us
    all_to_all x1, starting transfers between devices, on_device(): lax.all_to_all(cand_context.reshape(peer_count, per_owner, features), 'us...  6.86 us
    dot_general x1, matrix products, on_device(): jnp.dot(normed, kv_weight, preferred_element_type=jnp.float32)  4.92 us
    concatenate x2, local copies, waits for them, and re-layouts, on_device(): jnp.concatenate([history_queries, arrived], axis=0)  4.87 us
  transfers between devices with their start and end apart: 2, of which 2 were waited for; matrix products, arithmetic and copies ran while one was open for 16% of the time, Pallas kernels for 0%

commit v1 on v0

v1 whole, which is shorter than its diff:
```python
import functools

import jax
import jax.numpy as jnp
from jax import lax
from jax.experimental import pallas as pl
from jax.experimental.pallas import tpu as pltpu
from jax.sharding import PartitionSpec as P

HEADS = 16
LANES = 128
EPSILON = 1e-06
NEG = -1e30
F32 = jnp.float32
BF16 = jnp.bfloat16
MESH = pl.DeviceIdType.MESH


def normed_rows(values):
    values = values.astype(F32)
    mean = jnp.mean(values * values, axis=-1, keepdims=True)
    return (values * lax.rsqrt(mean + EPSILON)).astype(BF16)


def dot_t(a, b):
    return lax.dot_general(a, b, (((1,), (1,)), ((), ())), preferred_element_type=F32)


def dot(a, b):
    return jnp.dot(a, b, preferred_element_type=F32)


def kernel(
    peers,
    cap,
    chunk,
    len_ref,
    user_ref,
    task_ref,
    cand_ref,
    head_ref,
    hist_hbm,
    kvw_hbm,
    qw_hbm,
    ow_hbm,
    new_hbm,
    score_ref,
    hist,
    kvw,
    qw,
    ow,
    new,
    normed,
    keys,
    values,
    queries,
    context,
    bias,
    outbox,
    inbox,
    cand_queries,
    cand_context,
    logit_out,
    logit_in,
    load_sem,
    send_sem,
    recv_sem,
    back_send_sem,
    back_recv_sem,
):
    me = lax.axis_index("users")
    half_peers = peers // 2
    events, features = hist.shape
    slots = inbox.shape[0]
    rows = cand_ref.shape[0]
    pairs = features // LANES
    half = me // half_peers

    loads = [
        pltpu.make_async_copy(src, dst, load_sem.at[i])
        for i, (src, dst) in enumerate(
            ((hist_hbm.at[0], hist), (kvw_hbm, kvw), (qw_hbm, qw), (ow_hbm, ow))
        )
    ]
    for load in loads:
        load.start()

    barrier = pltpu.get_barrier_semaphore()

    def greet(i, carry):
        pl.semaphore_signal(
            barrier, inc=1, device_id={"users": lax.rem(me + i, peers)}, device_id_type=MESH
        )
        return carry

    lax.fori_loop(1, peers, greet, 0)

    row_id = lax.broadcasted_iota(jnp.int32, (rows, rows), 0)
    col_id = lax.broadcasted_iota(jnp.int32, (rows, rows), 1)
    eye = row_id == col_id
    user_row = user_ref[...].astype(F32)
    task_row = task_ref[...].astype(F32)
    user_col = jnp.sum(jnp.where(eye, user_row, 0.0), axis=1, keepdims=True)
    task_col = jnp.sum(jnp.where(eye, task_row, 0.0), axis=1, keepdims=True)
    same = user_col == user_row
    rank_row = jnp.sum(jnp.where(same & (row_id < col_id), 1.0, 0.0), axis=0, keepdims=True)
    rank_col = jnp.sum(jnp.where(same & (col_id < row_id), 1.0, 0.0), axis=1, keepdims=True)
    target_row = user_row * cap + rank_row

    def pack(first):
        slot = (lax.broadcasted_iota(jnp.int32, (chunk, rows), 0) + first).astype(F32)
        chosen = jnp.where(slot == target_row, 1.0, 0.0).astype(BF16)
        outbox[pl.ds(first, chunk), :] = dot(chosen, cand_ref[...]).astype(BF16)

    def block(ref, peer):
        return ref.at[pl.ds(pl.multiple_of(peer * cap, cap), cap), :]

    def sending(peer):
        return pltpu.make_async_remote_copy(
            src_ref=block(outbox, peer),
            dst_ref=block(inbox, me),
            send_sem=send_sem.at[peer],
            recv_sem=recv_sem.at[me],
            device_id={"users": peer},
            device_id_type=MESH,
        )

    def receiving(peer):
        return pltpu.make_async_remote_copy(
            src_ref=block(outbox, peer),
            dst_ref=block(inbox, peer),
            send_sem=send_sem.at[peer],
            recv_sem=recv_sem.at[peer],
            device_id={"users": peer},
            device_id_type=MESH,
        )

    half_chunks = slots // 2 // chunk
    far = 1 - half

    def pack_half(which):
        def step(i, carry):
            pack(pl.multiple_of(which * (slots // 2) + i * chunk, chunk))
            return carry

        lax.fori_loop(0, half_chunks, step, 0)

    pack_half(far)
    pl.semaphore_wait(barrier, peers - 1)

    def send_far(i, carry):
        sending(far * half_peers + lax.rem(me + i, half_peers)).start()
        return carry

    lax.fori_loop(0, half_peers, send_far, 0)
    pack_half(half)

    def send_near(i, carry):
        sending(half * half_peers + lax.rem(me + i, half_peers)).start()
        return carry

    lax.fori_loop(1, half_peers, send_near, 0)
    own = pl.ds(pl.multiple_of(me * cap, cap), cap)
    inbox[own, :] = outbox[own, :]

    loads[0].wait()
    normed[...] = normed_rows(hist[...])
    event_row = lax.broadcasted_iota(jnp.int32, (events, events), 0)
    event_col = lax.broadcasted_iota(jnp.int32, (events, events), 1)
    allowed = (event_col <= event_row) & (event_col < len_ref[0])
    bias[...] = jnp.where(allowed, 0.0, NEG)
    scale = 0.125
    low = lax.broadcasted_iota(jnp.int32, (events, LANES), 1) < LANES // 2
    loads[1].wait()
    loads[2].wait()

    def project(i, carry):
        cols = pl.ds(pl.multiple_of(i * 256, 256), 256)
        later = pl.ds(pl.multiple_of(features + i * 256, 256), 256)
        n = normed[...]
        k = dot(n, kvw[:, cols])
        v = dot(n, kvw[:, later])
        q = dot(n, qw[:, cols])
        queries[:, cols] = (q.astype(BF16).astype(F32) * scale).astype(BF16)
        for j in range(2):
            kk = k[:, j * LANES : (j + 1) * LANES]
            vv = v[:, j * LANES : (j + 1) * LANES]
            keys[4 * i + 2 * j] = jnp.where(low, kk, 0.0).astype(BF16)
            keys[4 * i + 2 * j + 1] = jnp.where(low, 0.0, kk).astype(BF16)
            values[4 * i + 2 * j] = jnp.where(low, vv, 1.0).astype(BF16)
            values[4 * i + 2 * j + 1] = jnp.where(low, 1.0, vv).astype(BF16)
        return carry

    lax.fori_loop(0, features // 256, project, 0)

    def attend(q2, head, count, offset):
        s = dot_t(q2, keys[head, :count, :]) + offset
        top = jnp.max(s, axis=1, keepdims=True)
        w = jnp.exp(s - top).astype(BF16)
        return dot(w, values[head, :count, :])

    def join(first, second):
        is_low = lax.broadcasted_iota(jnp.int32, first.shape, 1) < LANES // 2
        total = pltpu.roll(jnp.where(is_low, second, first), LANES // 2, 1)
        return (jnp.where(is_low, first, second) / total).astype(BF16)

    step_rows = 256

    def history_pair(p, carry):
        cols = pl.ds(pl.multiple_of(p * LANES, LANES), LANES)
        for r in range(0, events, step_rows):
            q2 = queries[r : r + step_rows, cols]
            count = r + step_rows
            offset = bias[r : r + step_rows, :count]
            context[r : r + step_rows, cols] = join(
                attend(q2, 2 * p, count, offset), attend(q2, 2 * p + 1, count, offset)
            )
        return carry

    lax.fori_loop(0, pairs, history_pair, 0)
    loads[3].wait()

    def history_out(i, carry):
        cols = pl.ds(pl.multiple_of(i * 256, 256), 256)
        new[:, cols] = (hist[:, cols].astype(F32) + dot(context[...], ow[:, cols])).astype(BF16)
        return carry

    lax.fori_loop(0, features // 256, history_out, 0)
    store = pltpu.make_async_copy(new, new_hbm.at[0], load_sem.at[4])
    store.start()

    chunks = slots // chunk
    per_chunk = chunk // cap

    def candidate_chunk(c, carry):
        which = lax.rem(half * (chunks // 2) + c, chunks)

        def arrive(i, inner):
            peer = which * per_chunk + i

            @pl.when(peer != me)
            def _():
                receiving(peer).wait_recv()

            return inner

        lax.fori_loop(0, per_chunk, arrive, 0)
        here = pl.ds(pl.multiple_of(which * chunk, chunk), chunk)
        n = normed_rows(inbox[here, :])
        q = dot(n, qw[...])
        cand_queries[...] = (q.astype(BF16).astype(F32) * scale).astype(BF16)

        def candidate_pair(p, inner):
            cols = pl.ds(pl.multiple_of(p * LANES, LANES), LANES)
            q2 = cand_queries[:, cols]
            offset = bias[events - 1 : events, :]
            cand_context[:, cols] = join(
                attend(q2, 2 * p, events, offset), attend(q2, 2 * p + 1, events, offset)
            )
            return inner

        lax.fori_loop(0, pairs, candidate_pair, 0)
        combined = inbox[here, :].astype(F32) + dot(cand_context[...], ow[...])
        logits = dot_t(head_ref[...], normed_rows(combined))
        for t in range(chunk // LANES):
            logit_out[which * (chunk // LANES) + t] = logits[:8, t * LANES : (t + 1) * LANES]
        return carry

    lax.fori_loop(0, chunks, candidate_chunk, 0)

    per_tile = LANES // cap

    def returning(peer):
        return pltpu.make_async_remote_copy(
            src_ref=logit_out.at[peer // per_tile],
            dst_ref=logit_in.at[me],
            send_sem=back_send_sem.at[peer],
            recv_sem=back_recv_sem.at[me],
            device_id={"users": peer},
            device_id_type=MESH,
        )

    def coming_back(peer):
        return pltpu.make_async_remote_copy(
            src_ref=logit_out.at[peer // per_tile],
            dst_ref=logit_in.at[peer],
            send_sem=back_send_sem.at[peer],
            recv_sem=back_recv_sem.at[peer],
            device_id={"users": peer},
            device_id_type=MESH,
        )

    def send_back(i, carry):
        returning(lax.rem(me + half_peers + i, peers)).start()
        return carry

    lax.fori_loop(0, half_peers, send_back, 0)

    def send_back_rest(i, carry):
        returning(lax.rem(me + i, peers)).start()
        return carry

    lax.fori_loop(1, half_peers, send_back_rest, 0)
    logit_in[me] = logit_out[me // per_tile]

    def back_arrive(i, carry):
        coming_back(lax.rem(me + i, peers)).wait_recv()
        return carry

    lax.fori_loop(1, peers, back_arrive, 0)

    lane = lax.broadcasted_iota(jnp.int32, (rows, LANES), 1).astype(F32)
    wanted = lane == rank_col + (lax.rem(me, per_tile) * cap).astype(F32)

    def pick(u, total):
        tile = logit_in[u]
        value = jnp.where(
            task_col == 0.0, tile[0:1], jnp.where(task_col == 1.0, tile[1:2], tile[2:3])
        )
        return jnp.where(user_col == u.astype(F32), value, total)

    picked = lax.fori_loop(0, peers, pick, jnp.zeros((rows, LANES), F32))
    score_col = jnp.sum(jnp.where(wanted, picked, 0.0), axis=1, keepdims=True)
    score_ref[...] = jnp.sum(jnp.where(eye, score_col, 0.0), axis=0, keepdims=True)

    def sent(i, carry):
        peer = lax.rem(me + i, peers)
        sending(peer).wait_send()
        returning(peer).wait_send()
        return carry

    lax.fori_loop(1, peers, sent, 0)
    store.wait()


def on_device(
    history,
    hist_len,
    candidates,
    cand_user,
    cand_task,
    kv_weight,
    query_weight,
    out_weight,
    head_weight,
):
    peers = lax.axis_size("users")
    rows, features = candidates.shape
    events = history.shape[1]
    cap = max(16, 2 * rows // peers)
    slots = peers * cap
    chunk = min(256, slots // 2)
    head_rows = jnp.pad(head_weight.T, ((0, 16 - head_weight.shape[1]), (0, 0)))
    vmem = pl.BlockSpec(memory_space=pltpu.VMEM)
    anywhere = pl.BlockSpec(memory_space=pl.ANY)
    new_history, scores = pl.pallas_call(
        functools.partial(kernel, peers, cap, chunk),
        out_shape=(
            jax.ShapeDtypeStruct(history.shape, history.dtype),
            jax.ShapeDtypeStruct((1, rows), F32),
        ),
        in_specs=[pl.BlockSpec(memory_space=pltpu.SMEM)] + [vmem] * 4 + [anywhere] * 4,
        out_specs=(anywhere, vmem),
        scratch_shapes=[
            pltpu.VMEM((events, features), BF16),
            pltpu.VMEM((features, 2 * features), BF16),
            pltpu.VMEM((features, features), BF16),
            pltpu.VMEM((features, features), BF16),
            pltpu.VMEM((events, features), BF16),
            pltpu.VMEM((events, features), BF16),
            pltpu.VMEM((HEADS, events, LANES), BF16),
            pltpu.VMEM((HEADS, events, LANES), BF16),
            pltpu.VMEM((events, features), BF16),
            pltpu.VMEM((events, features), BF16),
            pltpu.VMEM((events, events), F32),
            pltpu.VMEM((slots, features), BF16),
            pltpu.VMEM((slots, features), BF16),
            pltpu.VMEM((chunk, features), BF16),
            pltpu.VMEM((chunk, features), BF16),
            pltpu.VMEM((slots // LANES, 8, LANES), F32),
            pltpu.VMEM((peers, 8, LANES), F32),
            pltpu.SemaphoreType.DMA((5,)),
            pltpu.SemaphoreType.DMA((peers,)),
            pltpu.SemaphoreType.DMA((peers,)),
            pltpu.SemaphoreType.DMA((peers,)),
            pltpu.SemaphoreType.DMA((peers,)),
        ],
        compiler_params=pltpu.CompilerParams(
            collective_id=0, has_side_effects=True, vmem_limit_bytes=48 * 1024 * 1024
        ),
    )(
        hist_len,
        cand_user.reshape(1, rows),
        cand_task.reshape(1, rows),
        candidates,
        head_rows,
        history,
        kv_weight,
        query_weight,
        out_weight,
    )
    return new_history, scores.reshape(rows)


def solution(mesh):
    both = ("groups", "users")
    placed = (
        P(both, None, None),
        P(both),
        P(both, None),
        P(both, None),
        P(both),
        P(),
        P(),
        P(),
        P(),
    )
    return jax.shard_map(
        on_device,
        mesh=mesh,
        in_specs=placed,
        out_specs=(P(both, None, None), P(both)),
        check_vma=False,
    )
```

time: 155 us -> 55.9 us (0.36); the launches traced: 153 us -> 55.6 us
  matrix products: 48 us -> 0 us
  Pallas kernels: 0 us -> 46.8 us
  other arithmetic: 41.5 us -> 0 us
  waiting for transfers between devices: 21.3 us -> 0 us
  local copies, waits for them, and re-layouts: 26.5 us -> 7.45 us
  starting transfers between devices: 14.2 us -> 0 us
    dot_general x8 -> x0, matrix products: 48 us -> none  [the longest x1 17.2 us: attend(): jnp.einsum('rhd,khd->hrk', query_heads, key_heads, preferred_element_type...]
    pallas_call x0 -> x1, Pallas kernels: none -> 46.8 us  [on_device(): pl.pallas_call(functools.partial(kernel, peers, cap, chunk), out_shape=(j...]
    sub x2 -> x0, other arithmetic: 34.9 us -> none  [the longest x1 34.9 us: attend(): raised = jnp.exp(scores - highest)]
    all_to_all x2 -> x0, waiting for transfers between devices: 21.3 us -> none  [the longest x1 19.1 us: on_device(): lax.all_to_all(cand_context.reshape(peer_count, per_owner, features), 'us...]
    all_to_all x2 -> x0, starting transfers between devices: 14.2 us -> none  [the longest x1 7.37 us: on_device(): lax.all_to_all(blank_slots.at[target].set(cand_queries).reshape(peer_coun...]
    slice x6 -> x0, local copies, waits for them, and re-layouts: 10.4 us -> none  [the longest x2 4.14 us: on_device(): cand_context = context[events:]]
    unnamed x10 -> x12, local copies, waits for them, and re-layouts: 0.03 us -> 6.75 us
    concatenate x2 -> x0, local copies, waits for them, and re-layouts: 4.87 us -> none  [on_device(): jnp.concatenate([history_queries, arrived], axis=0)]
  transfers between devices with their start and end apart: 2 -> 0, of which waited for: 2 -> 0; matrix products, arithmetic and copies ran while one was open for 16% -> 0% of each run, Pallas kernels for 0% -> 0%
where the time goes in v1:
time: 55.9 us; the launch traced here: 55.6 us
  Pallas kernels  46.8 us (84%)
  local copies, waits for them, and re-layouts  7.45 us (13%)
  between operations  1.29 us (2%)
    pallas_call x1, Pallas kernels, on_device(): pl.pallas_call(functools.partial(kernel, peers, cap, chunk), out_shape=(j...  46.8 us
    unnamed x12, local copies, waits for them, and re-layouts  6.75 us

profile of v1, /device:TPU:0, one launch (start us, length us, event | category | flops | bytes accessed | tf_op | source)
XLA Modules:
  0.0 55.6 jit_solution(12558514682676823551)
XLA Ops:
  1.3 0.7 %pad.4.head_ref = bf16[16,1024]{1,0:T(8,128)(2,1)S(1)} pad(bf16[3,1024]{1,0:T(4,128)(2,1)} %bitcast.7, bf16[]{:T(256)} %constant.2.clone.1), padding=0_13x0_0 | pad | bytes 38914 | tf_op jit(solution)/shard_map/jit(_pad)/pad | solution.py:353
  2.0 0.0 copy-start
  2.0 1.6 %copy-done = bf16[1024,1024]{1,0:T(8,128)(2,1)S(1)} copy-done((bf16[1024,1024]{1,0:T(8,128)(2,1)S(1)}, bf16[1024,1024]{1,0:T(8,128)(2,1)}, u32[]{:S(2)}) %copy-start) | copy-done | bytes 2097176
  3.6 0.0 copy-start.1
  3.6 1.2 %copy-done.1 = bf16[1,512,1024]{2,1,0:T(8,128)(2,1)S(1)} copy-done((bf16[1,512,1024]{2,1,0:T(8,128)(2,1)S(1)}, bf16[1,512,1024]{2,1,0:T(8,128)(2,1)}, u32[]{:S(2)}) %copy-start.1) | copy-done | bytes 1048600
  4.8 0.0 copy-start.2
  4.8 1.0 %copy-done.2 = bf16[256,1024]{1,0:T(8,128)(2,1)S(1)} copy-done((bf16[256,1024]{1,0:T(8,128)(2,1)S(1)}, bf16[256,1024]{1,0:T(8,128)(2,1)}, u32[]{:S(2)}) %copy-start.2) | copy-done | bytes 524312
  5.8 0.0 copy-start.3
  5.8 0.7 %copy-done.3 = s32[256,1]{0,1:T(1,128)S(1)} copy-done((s32[256,1]{0,1:T(1,128)S(1)}, s32[256,1]{0,1:T(1,128)}, u32[]{:S(2)}) %copy-start.3) | copy-done | bytes 1048
  6.5 0.0 copy-start.4
  6.5 0.7 %copy-done.4 = s32[256]{0:T(256)S(1)} copy-done((s32[256]{0:T(256)S(1)}, s32[256]{0:T(256)}, u32[]{:S(2)}) %copy-start.4) | copy-done | bytes 1048
  7.2 46.8 %shard_map.104 = (bf16[1,512,1024]{2,1,0:T(8,128)(2,1)S(1)}, f32[1,256]{1,0:T(1,128)S(1)}) custom-call(s32[1]{0:T(128)S(6)} %copy.13.len_ref, s32[1,256]{1,0:T(1,128)S(1)} %bitcast.4, s32[1,256]{1,0:T(1,128)S(1)} %bitcast.5, bf16[256,1024]{1,0:T(8,128)(2,1)S(1)} %copy-done.2, bf16[16,1024]{1,0:T(8,128)(2,1)S(1)} %pad.4.head_ref, ...), custom_call_target="tpu_custom_call" | custom-call | tf_op jit(solution)/shard_map/pallas_call | solution.py:356
  54.0 1.0 %copy.14 = bf16[1,512,1024]{2,1,0:T(8,128)(2,1)} copy(bf16[1,512,1024]{2,1,0:T(8,128)(2,1)S(1)} %get-tuple-element.8) | data formatting | bytes 2097152
  55.0 0.6 %copy.15 = f32[256]{0:T(256)} copy(f32[256]{0:T(256)S(1)} %bitcast.6) | data formatting | bytes 2048
Async XLA Ops:
  2.0 1.6 %copy-start = (bf16[1024,1024]{1,0:T(8,128)(2,1)S(1)}, bf16[1024,1024]{1,0:T(8,128)(2,1)}, u32[]{:S(2)}) copy-start(bf16[1024,1024]{1,0:T(8,128)(2,1)} %qw_hbm.1) | copy-start | bytes 6291460
  3.6 1.2 %copy-start.1 = (bf16[1,512,1024]{2,1,0:T(8,128)(2,1)S(1)}, bf16[1,512,1024]{2,1,0:T(8,128)(2,1)}, u32[]{:S(2)}) copy-start(bf16[1,512,1024]{2,1,0:T(8,128)(2,1)} %hist_hbm.1) | copy-start | bytes 3145732
  4.8 1.0 %copy-start.2 = (bf16[256,1024]{1,0:T(8,128)(2,1)S(1)}, bf16[256,1024]{1,0:T(8,128)(2,1)}, u32[]{:S(2)}) copy-start(bf16[256,1024]{1,0:T(8,128)(2,1)} %cand_ref.1) | copy-start | bytes 1572868
  5.8 0.7 %copy-start.3 = (s32[256,1]{0,1:T(1,128)S(1)}, s32[256,1]{0,1:T(1,128)}, u32[]{:S(2)}) copy-start(s32[256,1]{0,1:T(1,128)} %param.12) | copy-start | bytes 3076
  6.5 0.7 %copy-start.4 = (s32[256]{0:T(256)S(1)}, s32[256]{0:T(256)}, u32[]{:S(2)}) copy-start(s32[256]{0:T(256)} %param.13) | copy-start | bytes 3076

commit v2 on v1

--- a/solution.py
+++ b/solution.py
@@ -35,16 +35,20 @@
     cap,
     chunk,
     len_ref,
-    user_ref,
-    task_ref,
-    cand_ref,
-    head_ref,
+    user_hbm,
+    task_hbm,
+    cand_hbm,
+    head_hbm,
     hist_hbm,
     kvw_hbm,
     qw_hbm,
     ow_hbm,
     new_hbm,
     score_ref,
+    user_ref,
+    task_ref,
+    cand_ref,
+    head_ref,
     hist,
     kvw,
     qw,
@@ -74,12 +78,21 @@
     slots = inbox.shape[0]
     rows = cand_ref.shape[0]
     pairs = features // LANES
-    half = me // half_peers
+    tasks = head_ref.shape[0]
 
     loads = [
         pltpu.make_async_copy(src, dst, load_sem.at[i])
         for i, (src, dst) in enumerate(
-            ((hist_hbm.at[0], hist), (kvw_hbm, kvw), (qw_hbm, qw), (ow_hbm, ow))
+            (
+                (user_hbm, user_ref),
+                (task_hbm, task_ref),
+                (cand_hbm, cand_ref),
+                (hist_hbm.at[0], hist),
+                (kvw_hbm, kvw),
+                (qw_hbm, qw),
+                (ow_hbm, ow),
+                (head_hbm, head_ref),
+            )
         )
     ]
     for load in loads:
@@ -95,6 +108,8 @@
 
     lax.fori_loop(1, peers, greet, 0)
 
+    loads[0].wait()
+    loads[1].wait()
     row_id = lax.broadcasted_iota(jnp.int32, (rows, rows), 0)
     col_id = lax.broadcasted_iota(jnp.int32, (rows, rows), 1)
     eye = row_id == col_id
@@ -135,35 +150,52 @@
             device_id_type=MESH,
         )
 
-    half_chunks = slots // 2 // chunk
-    far = 1 - half
-
-    def pack_half(which):
-        def step(i, carry):
-            pack(pl.multiple_of(which * (slots // 2) + i * chunk, chunk))
+    groups = slots // chunk
+    members = peers // groups
+    part = groups // 2
+    group = me // members
+    group_half, group_rest = group // part, lax.rem(group, part)
+
+    def partner(phase, sign):
+        side = lax.rem(group_half + phase // part, 2)
+        return side * part + lax.rem(group_rest + part + sign * lax.rem(phase, part), part)
+
+    loads[2].wait()
+
+    def pack_phase(phase):
+        pack(pl.multiple_of(partner(phase, 1) * chunk, chunk))
+
+    def send_phase(phase):
+        first = partner(phase, 1) * members
+
+        def send_one(i, carry):
+            peer = first + lax.rem(me + i, members)
+
+            @pl.when(peer != me)
+            def _():
+                sending(peer).start()
+
             return carry
 
-        lax.fori_loop(0, half_chunks, step, 0)
-
-    pack_half(far)
+        lax.fori_loop(0, members, send_one, 0)
+
+    def order(i):
+        return lax.rem(i + part, groups)
+
+    pack_phase(order(0))
     pl.semaphore_wait(barrier, peers - 1)
-
-    def send_far(i, carry):
-        sending(far * half_peers + lax.rem(me + i, half_peers)).start()
-        return carry
-
-    lax.fori_loop(0, half_peers, send_far, 0)
-    pack_half(half)
-
-    def send_near(i, carry):
-        sending(half * half_peers + lax.rem(me + i, half_peers)).start()
-        return carry
-
-    lax.fori_loop(1, half_peers, send_near, 0)
+    send_phase(order(0))
+
+    def pack_and_send(i, carry):
+        pack_phase(order(i))
+        send_phase(order(i))
+        return carry
+
+    lax.fori_loop(1, groups, pack_and_send, 0)
     own = pl.ds(pl.multiple_of(me * cap, cap), cap)
     inbox[own, :] = outbox[own, :]
 
-    loads[0].wait()
+    loads[3].wait()
     normed[...] = normed_rows(hist[...])
     event_row = lax.broadcasted_iota(jnp.int32, (events, events), 0)
     event_col = lax.broadcasted_iota(jnp.int32, (events, events), 1)
@@ -171,8 +203,8 @@
     bias[...] = jnp.where(allowed, 0.0, NEG)
     scale = 0.125
     low = lax.broadcasted_iota(jnp.int32, (events, LANES), 1) < LANES // 2
-    loads[1].wait()
-    loads[2].wait()
+    loads[4].wait()
+    loads[5].wait()
 
     def project(i, carry):
         cols = pl.ds(pl.multiple_of(i * 256, 256), 256)
@@ -187,8 +219,8 @@
             vv = v[:, j * LANES : (j + 1) * LANES]
             keys[4 * i + 2 * j] = jnp.where(low, kk, 0.0).astype(BF16)
             keys[4 * i + 2 * j + 1] = jnp.where(low, 0.0, kk).astype(BF16)
-            values[4 * i + 2 * j] = jnp.where(low, vv, 1.0).astype(BF16)
-            values[4 * i + 2 * j + 1] = jnp.where(low, 1.0, vv).astype(BF16)
+            values[4 * i + 2 * j] = jnp.where(low, vv, 0.0).astype(BF16)
+            values[4 * i + 2 * j + 1] = jnp.where(low, 0.0, vv).astype(BF16)
         return carry
 
     lax.fori_loop(0, features // 256, project, 0)
@@ -196,13 +228,13 @@
     def attend(q2, head, count, offset):
         s = dot_t(q2, keys[head, :count, :]) + offset
         top = jnp.max(s, axis=1, keepdims=True)
-        w = jnp.exp(s - top).astype(BF16)
-        return dot(w, values[head, :count, :])
-
-    def join(first, second):
-        is_low = lax.broadcasted_iota(jnp.int32, first.shape, 1) < LANES // 2
-        total = pltpu.roll(jnp.where(is_low, second, first), LANES // 2, 1)
-        return (jnp.where(is_low, first, second) / total).astype(BF16)
+        raised = jnp.exp(s - top)
+        share = 1.0 / jnp.sum(raised, axis=1, keepdims=True)
+        return dot((raised * share).astype(BF16), values[head, :count, :])
+
+    def attend_pair(q2, p, count, offset):
+        both = attend(q2, 2 * p, count, offset) + attend(q2, 2 * p + 1, count, offset)
+        return both.astype(BF16)
 
     step_rows = 256
 
@@ -212,13 +244,11 @@
             q2 = queries[r : r + step_rows, cols]
             count = r + step_rows
             offset = bias[r : r + step_rows, :count]
-            context[r : r + step_rows, cols] = join(
-                attend(q2, 2 * p, count, offset), attend(q2, 2 * p + 1, count, offset)
-            )
-        return carry
-
-    lax.fori_loop(0, pairs, history_pair, 0)
-    loads[3].wait()
+            context[r : r + step_rows, cols] = attend_pair(q2, p, count, offset)
+        return carry
+
+    lax.fori_loop(0, pairs, history_pair, 0, unroll=4)
+    loads[6].wait()
 
     def history_out(i, carry):
         cols = pl.ds(pl.multiple_of(i * 256, 256), 256)
@@ -226,17 +256,16 @@
         return carry
 
     lax.fori_loop(0, features // 256, history_out, 0)
-    store = pltpu.make_async_copy(new, new_hbm.at[0], load_sem.at[4])
+    store = pltpu.make_async_copy(new, new_hbm.at[0], load_sem.at[8])
     store.start()
 
-    chunks = slots // chunk
-    per_chunk = chunk // cap
+    loads[7].wait()
 
     def candidate_chunk(c, carry):
-        which = lax.rem(half * (chunks // 2) + c, chunks)
+        which = partner(c, -1)
 
         def arrive(i, inner):
-            peer = which * per_chunk + i
+            peer = which * members + i
 
             @pl.when(peer != me)
             def _():
@@ -244,7 +273,7 @@
 
             return inner
 
-        lax.fori_loop(0, per_chunk, arrive, 0)
+        lax.fori_loop(0, members, arrive, 0)
         here = pl.ds(pl.multiple_of(which * chunk, chunk), chunk)
         n = normed_rows(inbox[here, :])
         q = dot(n, qw[...])
@@ -254,19 +283,19 @@
             cols = pl.ds(pl.multiple_of(p * LANES, LANES), LANES)
             q2 = cand_queries[:, cols]
             offset = bias[events - 1 : events, :]
-            cand_context[:, cols] = join(
-                attend(q2, 2 * p, events, offset), attend(q2, 2 * p + 1, events, offset)
-            )
+            cand_context[:, cols] = attend_pair(q2, p, events, offset)
             return inner
 
-        lax.fori_loop(0, pairs, candidate_pair, 0)
+        lax.fori_loop(0, pairs, candidate_pair, 0, unroll=4)
         combined = inbox[here, :].astype(F32) + dot(cand_context[...], ow[...])
         logits = dot_t(head_ref[...], normed_rows(combined))
         for t in range(chunk // LANES):
-            logit_out[which * (chunk // LANES) + t] = logits[:8, t * LANES : (t + 1) * LANES]
-        return carry
-
-    lax.fori_loop(0, chunks, candidate_chunk, 0)
+            logit_out[which * (chunk // LANES) + t, :tasks, :] = logits[
+                :, t * LANES : (t + 1) * LANES
+            ]
+        return carry
+
+    lax.fori_loop(0, groups, candidate_chunk, 0)
 
     per_tile = LANES // cap
 
@@ -349,8 +378,7 @@
     events = history.shape[1]
     cap = max(16, 2 * rows // peers)
     slots = peers * cap
-    chunk = min(256, slots // 2)
-    head_rows = jnp.pad(head_weight.T, ((0, 16 - head_weight.shape[1]), (0, 0)))
+    chunk = 256
     vmem = pl.BlockSpec(memory_space=pltpu.VMEM)
     anywhere = pl.BlockSpec(memory_space=pl.ANY)
     new_history, scores = pl.pallas_call(
@@ -359,9 +387,13 @@
             jax.ShapeDtypeStruct(history.shape, history.dtype),
             jax.ShapeDtypeStruct((1, rows), F32),
         ),
-        in_specs=[pl.BlockSpec(memory_space=pltpu.SMEM)] + [vmem] * 4 + [anywhere] * 4,
+        in_specs=[pl.BlockSpec(memory_space=pltpu.SMEM)] + [anywhere] * 8,
         out_specs=(anywhere, vmem),
         scratch_shapes=[
+            pltpu.VMEM((1, rows), jnp.int32),
+            pltpu.VMEM((1, rows), jnp.int32),
+            pltpu.VMEM((rows, features), BF16),
+            pltpu.VMEM((head_weight.shape[1], features), BF16),
             pltpu.VMEM((events, features), BF16),
             pltpu.VMEM((features, 2 * features), BF16),
             pltpu.VMEM((features, features), BF16),
@@ -379,21 +411,21 @@
             pltpu.VMEM((chunk, features), BF16),
             pltpu.VMEM((slots // LANES, 8, LANES), F32),
             pltpu.VMEM((peers, 8, LANES), F32),
-            pltpu.SemaphoreType.DMA((5,)),
+            pltpu.SemaphoreType.DMA((9,)),
             pltpu.SemaphoreType.DMA((peers,)),
             pltpu.SemaphoreType.DMA((peers,)),
             pltpu.SemaphoreType.DMA((peers,)),
             pltpu.SemaphoreType.DMA((peers,)),
         ],
         compiler_params=pltpu.CompilerParams(
-            collective_id=0, has_side_effects=True, vmem_limit_bytes=48 * 1024 * 1024
+            collective_id=0, has_side_effects=True, vmem_limit_bytes=60 * 1024 * 1024
         ),
     )(
         hist_len,
         cand_user.reshape(1, rows),
         cand_task.reshape(1, rows),
         candidates,
-        head_rows,
+        head_weight.T,
         history,
         kv_weight,
         query_weight,

time: 55.9 us -> 49.2 us (0.88)
  local copies, waits for them, and re-layouts: 7.45 us -> 2.83 us
  Pallas kernels: 46.8 us -> 44.9 us
    unnamed x12 -> x4, local copies, waits for them, and re-layouts: 6.75 us -> 2.83 us
    pallas_call x1, Pallas kernels: 46.8 us -> 44.9 us  [on_device(): pl.pallas_call(functools.partial(kernel, peers, cap, chunk), out_shape=(j...]
    pad x1 -> x0, local copies, waits for them, and re-layouts: 0.71 us -> none  [on_device(): head_rows = jnp.pad(head_weight.T, ((0, 16 - head_weight.shape[1]), (0, 0)))]
where the time goes in v2:
time: 49.2 us; the launch traced here: 49 us
  Pallas kernels  44.9 us (91%)
  local copies, waits for them, and re-layouts  2.83 us (6%)
  between operations  1.29 us (3%)
    pallas_call x1, Pallas kernels, on_device(): pl.pallas_call(functools.partial(kernel, peers, cap, chunk), out_shape=(j...  44.9 us
    unnamed x4, local copies, waits for them, and re-layouts  2.83 us

profile of v2, /device:TPU:0, one launch (start us, length us, event | category | flops | bytes accessed | tf_op | source)
XLA Modules:
  0.0 49.0 jit_solution(17917191406042152792)
XLA Ops:
  1.3 44.9 %shard_map.104 = (bf16[1,512,1024]{2,1,0:T(8,128)(2,1)}, f32[1,256]{1,0:T(1,128)}) custom-call(s32[1]{0:T(128)S(6)} %copy.13.len_ref, s32[1,256]{1,0:T(1,128)} %bitcast.5, s32[1,256]{1,0:T(1,128)} %bitcast.6, bf16[256,1024]{1,0:T(8,128)(2,1)} %cand_hbm.1, bf16[3,1024]{1,0:T(4,128)(2,1)} %bitcast.4, bf16[1,512,1024]{2,1,0:T(8,128)(2,1)} %hist_hbm.1, ...), custom_call_target="tpu_custom_call" | custom-call | tf_op jit(solution)/shard_map/pallas_call | solution.py:384
  46.2 0.0 copy-start
  46.2 2.3 %copy.14 = bf16[1,512,1024]{2,1,0:T(8,128)(2,1)} copy(bf16[1,512,1024]{2,1,0:T(8,128)(2,1)} %get-tuple-element.8) | data formatting | bytes 2097152
  48.4 0.0 copy-done
  48.4 0.6 %copy.15 = f32[256]{0:T(256)} copy(f32[256]{0:T(256)S(1)} %bitcast.7) | data formatting | bytes 2048
Async XLA Ops:
  46.2 2.3 %copy-start = (f32[1,256]{1,0:T(1,128)S(1)}, f32[1,256]{1,0:T(1,128)}, u32[]{:S(2)}) copy-start(f32[1,256]{1,0:T(1,128)} %get-tuple-element.5) | copy-start | bytes 3076

commit v3 on v2

--- a/solution.py
+++ b/solution.py
@@ -180,7 +180,7 @@
         lax.fori_loop(0, members, send_one, 0)
 
     def order(i):
-        return lax.rem(i + part, groups)
+        return i
 
     pack_phase(order(0))
     pl.semaphore_wait(barrier, peers - 1)
@@ -233,8 +233,16 @@
         return dot((raised * share).astype(BF16), values[head, :count, :])
 
     def attend_pair(q2, p, count, offset):
-        both = attend(q2, 2 * p, count, offset) + attend(q2, 2 * p + 1, count, offset)
-        return both.astype(BF16)
+        parts = []
+        for head in (2 * p, 2 * p + 1):
+            s = dot_t(q2, keys[head, :count, :]) + offset
+            raised = jnp.exp(s - jnp.max(s, axis=1, keepdims=True))
+            share = 1.0 / jnp.sum(raised, axis=1, keepdims=True)
+            parts.append((raised * share).astype(BF16))
+        pair_values = jnp.concatenate(
+            [values[2 * p, :count, :], values[2 * p + 1, :count, :]], axis=0
+        )
+        return dot(jnp.concatenate(parts, axis=1), pair_values).astype(BF16)
 
     step_rows = 256
 
@@ -247,7 +255,7 @@
             context[r : r + step_rows, cols] = attend_pair(q2, p, count, offset)
         return carry
 
-    lax.fori_loop(0, pairs, history_pair, 0, unroll=4)
+    lax.fori_loop(0, pairs, history_pair, 0, unroll=8)
     loads[6].wait()
 
     def history_out(i, carry):
@@ -286,7 +294,7 @@
             cand_context[:, cols] = attend_pair(q2, p, events, offset)
             return inner
 
-        lax.fori_loop(0, pairs, candidate_pair, 0, unroll=4)
+        lax.fori_loop(0, pairs, candidate_pair, 0, unroll=8)
         combined = inbox[here, :].astype(F32) + dot(cand_context[...], ow[...])
         logits = dot_t(head_ref[...], normed_rows(combined))
         for t in range(chunk // LANES):

time: 49.2 us -> 47.3 us (0.961)
  Pallas kernels: 44.9 us -> 43 us
    pallas_call x1, Pallas kernels: 44.9 us -> 43 us  [on_device(): pl.pallas_call(functools.partial(kernel, peers, cap, chunk), out_shape=(j...]
where the time goes in v3:
time: 47.3 us; the launch traced here: 47.1 us
  Pallas kernels  43 us (91%)
  local copies, waits for them, and re-layouts  2.83 us (6%)
  between operations  1.3 us (3%)
    pallas_call x1, Pallas kernels, on_device(): pl.pallas_call(functools.partial(kernel, peers, cap, chunk), out_shape=(j...  43 us
    unnamed x4, local copies, waits for them, and re-layouts  2.83 us

profile of v3, /device:TPU:0, one launch (start us, length us, event | category | flops | bytes accessed | tf_op | source)
XLA Modules:
  0.0 47.1 jit_solution(453601069586110610)
XLA Ops:
  1.3 43.0 %shard_map.104 = (bf16[1,512,1024]{2,1,0:T(8,128)(2,1)}, f32[1,256]{1,0:T(1,128)}) custom-call(s32[1]{0:T(128)S(6)} %copy.13.len_ref, s32[1,256]{1,0:T(1,128)} %bitcast.5, s32[1,256]{1,0:T(1,128)} %bitcast.6, bf16[256,1024]{1,0:T(8,128)(2,1)} %cand_hbm.1, bf16[3,1024]{1,0:T(4,128)(2,1)} %bitcast.4, bf16[1,512,1024]{2,1,0:T(8,128)(2,1)} %hist_hbm.1, ...), custom_call_target="tpu_custom_call" | custom-call | tf_op jit(solution)/shard_map/pallas_call | solution.py:392
  44.3 0.0 copy-start
  44.3 2.3 %copy.14 = bf16[1,512,1024]{2,1,0:T(8,128)(2,1)} copy(bf16[1,512,1024]{2,1,0:T(8,128)(2,1)} %get-tuple-element.8) | data formatting | bytes 2097152
  46.5 0.0 copy-done
  46.5 0.6 %copy.15 = f32[256]{0:T(256)} copy(f32[256]{0:T(256)S(1)} %bitcast.7) | data formatting | bytes 2048
Async XLA Ops:
  44.3 2.3 %copy-start = (f32[1,256]{1,0:T(1,128)S(1)}, f32[1,256]{1,0:T(1,128)}, u32[]{:S(2)}) copy-start(f32[1,256]{1,0:T(1,128)} %get-tuple-element.5) | copy-start | bytes 3076
